TPU v7x, 128 devices: a whole 4x4x4 slice. The times are simulated.
128 devices in a mesh: dp: 16 (over z, x), fsdp: 8 (over y, core).
Axes of the slice: x: 4, y: 4, z: 4, core: 2. Of those that a mesh axis runs over, the one named last changes fastest.
Arguments:
- feats: bfloat16 [256, 1024, 96], P(('dp', 'fsdp')), may hold values from -6 to 6
- targets: float32 [256, 1024], P(('dp', 'fsdp')), may hold values from -36 to 36
- lag_mask: int32 [256, 84], P(('dp', 'fsdp')), may hold values 0 or 1
- date_mask: int32 [256, 12], P(('dp', 'fsdp')), may hold values 0 or 1
- freq_ids: int32 [256], P(('dp', 'fsdp')), may hold values from 0 to 2
- dataset_ids: int32 [256], P(('dp', 'fsdp')), may hold values from 0 to 7
- w_in: bfloat16 [13824], P(('dp', 'fsdp')), may hold values from -0.625 to 0.625
- w_qkv: bfloat16 [62208], P(('dp', 'fsdp')), may hold values from -0.5 to 0.5
- w_out: bfloat16 [20736], P(('dp', 'fsdp')), may hold values from -2 to 2
- w_gu: bfloat16 [147456], P(('dp', 'fsdp')), may hold values from -0.5 to 0.5
- w_down: bfloat16 [73728], P(('dp', 'fsdp')), may hold values from -0.25 to 0.25
- gains: bfloat16 [2, 144], P(None, 'dp'), may hold values from 0.5 to 1.5
- running: float32 [8], replicated, may hold values from 0.5 to 4
- d_out: bfloat16 [256, 1024, 144], P(('dp', 'fsdp')), may hold values from -6 to 6
Outputs:
- out: bfloat16 [256, 1024, 144], P(('dp', 'fsdp'))
- grad_feats: bfloat16 [256, 1024, 96], P(('dp', 'fsdp'))
- grad_w_in: float32 [13824], P(('dp', 'fsdp'))
- grad_w_qkv: float32 [62208], P(('dp', 'fsdp'))
- grad_w_out: float32 [20736], P(('dp', 'fsdp'))
- grad_w_gu: float32 [147456], P(('dp', 'fsdp'))
- grad_w_down: float32 [73728], P(('dp', 'fsdp'))
- grad_gains: float32 [2, 144], P(None, 'dp')
- running_next: float32 [8], replicated
All inputs are finite; a program needn't handle non-finite values. Where the computation divides by a largest or mean magnitude, that divisor is 1e-20 or more. No bound on the sum of `lag_mask` or of `date_mask` on one device may be relied on, other than what follows from the above.
Results may differ from a plain program's by a relative error of at most 0.014.
Values may be sent and summed in bfloat16 or wider, within the bound.
A program may use at most 256 MiB of HBM per device.

v0:
```python
import functools

import jax
import jax.numpy as jnp
import numpy as np
from jax import lax
from jax.experimental import pallas as pl
from jax.experimental.pallas import tpu as pltpu
from jax.sharding import PartitionSpec as P

D, H, HD, FF, NDATE, NLAG, F, NSET, LEN = 144, 9, 16, 512, 12, 84, 96, 8, 1024
EPS = 1e-05
TOK_IN = 1024
TOK_MLP = 1024
TOK_BACK = 1024
QT = 256
CH = 128
GROUP = 3
f32, bf16 = jnp.float32, jnp.bfloat16
MESH = pl.DeviceIdType.MESH
BOTH = ("dp", "fsdp")

A_ROWS, B_ROWS = 8, 16
SPECS = {
    "in": (D, 108, 4, 3, "a", 0),
    "qkv": (3 * D, 486, 8, 9, "a", 1),
    "gu": (2 * FF, 1152, 8, 9, "b", 0),
    "down": (D, 576, 2, 8, "b", 9),
    "out": (D, 162, 8, 9, "b", 14),
}
ROWS = {"in": F, "qkv": D, "gu": D, "down": FF, "out": D}


def dot(a, b, ca=1, cb=0, **kw):
    return lax.dot_general(a, b, (((ca,), (cb,)), ((), ())), preferred_element_type=f32, **kw)


def lane_tiles(width):
    return [(t // 128, t, min(128, width - t)) for t in range(0, width, 128)]


def pieces(piece, source, count):
    cuts = []
    for i in range(count):
        at, left, parts = i * piece, piece, []
        while left:
            c, o = divmod(at, source)
            n = min(left, source - o)
            parts.append((c, o, n))
            at, left = at + n, left - n
        cuts.append(parts)
    return cuts


def spot(c):
    return (c % 2) * 64 + c // 2


def join(parts):
    return parts[0] if len(parts) == 1 else jnp.concatenate(parts, axis=1)


def unpack(flat, rows, name, dst):
    cols, chunk, gc, gr, _, base = SPECS[name]
    groups, kept = 128 // gc, {}

    def owner(c):
        if c not in kept:
            kept[c] = join(
                [flat[pl.ds(spot(c) * rows + base + t, groups, stride=gc // 2 * rows), :] for t, _, _ in lane_tiles(chunk)]
            )
        return kept[c]

    for i, parts in enumerate(pieces(cols, chunk, gr)):
        row = join([owner(c)[:, o : o + n] for c, o, n in parts])
        for t, at, width in lane_tiles(cols):
            dst[t, pl.ds(i, groups, stride=gr), :width] = row[:, at : at + width]


def pack(src, name, flat, rows):
    cols, chunk, gc, gr, _, base = SPECS[name]
    groups, kept = 128 // gc, {}

    def line(i):
        if i not in kept:
            kept[i] = join([src[t, pl.ds(i, groups, stride=gr), :] for t, _, _ in lane_tiles(cols)])
        return kept[i]

    for c, parts in enumerate(pieces(chunk, cols, gc)):
        run = [line(i)[:, o : o + n] for i, o, n in parts]
        run = join(run + ([jnp.zeros((groups, -chunk % 128), f32)] if chunk % 128 else []))
        for t, at, _ in lane_tiles(chunk):
            flat[pl.ds(spot(c) * rows + base + t, groups, stride=gc // 2 * rows), :] = run[:, at : at + 128]


def place():
    fs = lax.axis_index("fsdp")
    return lax.axis_index("dp"), fs // 2, fs % 2


def partners():
    dp, y, core = place()
    across = lambda o: (lax.rem(dp + o, 16), 2 * y + core)
    along = lambda o: (dp, 2 * lax.rem(y + o, 4) + core)
    return across, along, (dp, 2 * y + 1 - core)


def chip(dz, dx, dy):
    dp, y, _ = place()
    z, x = dp // 4, lax.rem(dp, 4)
    return 4 * lax.rem(z + dz, 4) + lax.rem(x + dx, 4), lax.rem(y + dy, 4)


def device(dz, dx, dy):
    dp, y = chip(dz, dx, dy)
    return dp, 2 * y + place()[2]


STEPS = (1, 2, 3)
LINES = [(0, 0, o) for o in STEPS] + [(0, o, 0) for o in STEPS] + [(o, 0, 0) for o in STEPS]
X_PLANES = [(0, o, p) for o in STEPS for p in STEPS] + [(p, o, 0) for o in STEPS for p in STEPS]
REST = [(o, p, r) for o in STEPS for p in STEPS for r in STEPS] + [(o, 0, p) for o in STEPS for p in STEPS]


def signal(sem, to):
    pl.semaphore_signal(sem, inc=1, device_id=to, device_id_type=MESH)


def knock():
    barrier = pltpu.get_barrier_semaphore()
    for line in LINES:
        signal(barrier, device(*line))
    signal(barrier, partners()[2])


def enter(sem_x, sem_z, send_to, work):
    pl.semaphore_wait(pltpu.get_barrier_semaphore(), 10)
    for o in STEPS:
        signal(sem_x, device(0, o, 0))
    for line in LINES:
        send_to(*line)
    work[0]()
    pl.semaphore_wait(sem_x, 3)
    for o in STEPS:
        signal(sem_z, device(o, 0, 0))
    for line in X_PLANES:
        send_to(*line)
    work[1]()
    pl.semaphore_wait(sem_z, 3)
    for line in REST:
        send_to(*line)


def send(src, dst, sems, k, to):
    pltpu.make_async_remote_copy(
        src_ref=src, dst_ref=dst, send_sem=sems.at[0, k], recv_sem=sems.at[1, k], device_id=to, device_id_type=MESH
    ).start()


def wait(ref, sem):
    pltpu.make_async_copy(ref, ref, sem).wait()


class GatherDirect:
    def __init__(self, own, everyone, sems):
        self.own, self.all, self.sems = own, everyone, sems

    def to(self, *line):
        dp, y, core = place()
        send(self.own, self.all.at[core, 4 * dp + y], self.sems, 0, device(*line))

    def second(self):
        dp, y, core = place()
        self.all[core, 4 * dp + y] = self.own[...]
        wait(self.all.at[core, pl.ds(0, 63)], self.sems.at[1, 0])
        wait(self.all.at[core, pl.ds(0, 63)], self.sems.at[0, 0])
        send(self.all.at[core], self.all.at[core], self.sems, 1, partners()[2])

    def last(self):
        _, _, core = place()
        wait(self.all.at[core], self.sems.at[1, 1])
        wait(self.all.at[core], self.sems.at[0, 1])


class ReduceDirect:
    def __init__(self, parts, half, got, sems):
        self.parts, self.half, self.got, self.sems = parts, half, got, sems

    def first(self):
        _, _, core = place()
        send(self.parts.at[1 - core], self.half, self.sems, 0, partners()[2])

    def second(self):
        dp, y, core = place()
        wait(self.half, self.sems.at[1, 0])
        wait(self.half, self.sems.at[0, 0])
        self.half[...] += self.parts[core]
        for line in REST + X_PLANES + LINES:
            to_dp, to_y = chip(*line)
            send(self.half.at[4 * to_dp + to_y], self.got.at[4 * dp + y], self.sems, 1, device(*line))
        self.got[4 * dp + y] = self.half[4 * dp + y]

    def last(self):
        wait(self.got.at[pl.ds(0, 63)], self.sems.at[1, 1])
        wait(self.got.at[pl.ds(0, 63)], self.sems.at[0, 1])
        return jnp.sum(self.got[...], axis=0)


class Gather:
    def __init__(self, own, everyone, sems):
        self.own, self.all, self.sems = own, everyone, sems

    def first(self):
        dp, y, core = place()
        _, along, _ = partners()
        for o in (1, 2, 3):
            send(self.own, self.all.at[core, dp, y], self.sems, 0, along(o))
        self.all[core, dp, y] = self.own[...]

    def second(self):
        dp, y, core = place()
        across, _, _ = partners()
        wait(self.all.at[core, dp, pl.ds(0, 3)], self.sems.at[1, 0])
        wait(self.all.at[core, dp, pl.ds(0, 3)], self.sems.at[0, 0])
        line = self.all.at[core, dp]

        @pl.loop(1, 16)
        def _(o):
            send(line, line, self.sems, 1, across(o))

    def third(self):
        _, _, core = place()
        _, _, sibling = partners()
        wait(self.all.at[core, pl.ds(0, 15)], self.sems.at[1, 1])
        wait(self.all.at[core, pl.ds(0, 15)], self.sems.at[0, 1])
        send(self.all.at[core], self.all.at[core], self.sems, 2, sibling)

    def last(self):
        _, _, core = place()
        wait(self.all.at[core], self.sems.at[1, 2])
        wait(self.all.at[core], self.sems.at[0, 2])


class Reduce:
    def __init__(self, parts, half, row, line, sems):
        self.parts, self.half, self.row, self.line, self.sems = parts, half, row, line, sems

    def first(self):
        _, _, core = place()
        _, _, sibling = partners()
        send(self.parts.at[1 - core], self.half, self.sems, 0, sibling)

    def second(self):
        dp, y, core = place()
        across, _, _ = partners()
        wait(self.half, self.sems.at[1, 0])
        wait(self.half, self.sems.at[0, 0])
        self.half[...] = (self.half[...].astype(f32) + self.parts[core].astype(f32)).astype(self.half.dtype)

        @pl.loop(1, 16)
        def _(o):
            send(self.half.at[lax.rem(dp + o, 16)], self.row.at[dp], self.sems, 1, across(o))

        self.row[dp] = self.half[dp]

    def third(self):
        dp, y, core = place()
        _, along, _ = partners()
        wait(self.row.at[pl.ds(0, 15)], self.sems.at[1, 1])
        wait(self.row.at[pl.ds(0, 15)], self.sems.at[0, 1])
        mine = jnp.sum(self.row[...].astype(f32), axis=0).astype(self.row.dtype)
        self.half[0] = mine
        for o in (1, 2, 3):
            send(self.half.at[0, lax.rem(y + o, 4)], self.line.at[y], self.sems, 2, along(o))
        self.line[y] = self.half[0, y]

    def last(self):
        wait(self.line.at[pl.ds(0, 3)], self.sems.at[1, 2])
        wait(self.line.at[pl.ds(0, 3)], self.sems.at[0, 2])
        return jnp.sum(self.line[...].astype(f32), axis=0)


def rope_tables():
    freqs = np.float32(10000.0) ** (-np.arange(HD // 2, dtype=np.float32) * np.float32(2.0) / np.float32(HD))
    angle = np.arange(LEN, dtype=np.float32)[None, :] * freqs.astype(np.float32)[:, None]
    return np.cos(angle.astype(np.float64)).astype(np.float32), np.sin(angle.astype(np.float64)).astype(np.float32)


def own_tiles(w_in, w_qkv, w_out, w_gu, w_down, gains, tile_a, tile_b, wide):
    tile_a[...] = jnp.zeros_like(tile_a)
    wide[...] = jnp.zeros_like(wide)
    for name, ref in (("in", w_in), ("qkv", w_qkv), ("out", w_out), ("gu", w_gu), ("down", w_down)):
        _, chunk, _, _, which, base = SPECS[name]
        for t, at, width in lane_tiles(chunk):
            (tile_a if which == "a" else wide)[base + t, :width] = ref[pl.ds(at, width)].astype(f32)
    tile_a[0:1, 108:117] = gains[0:1, :].astype(f32)
    tile_a[0:1, 117:126] = gains[1:2, :].astype(f32)
    tile_b[...] = wide[...].astype(bf16)


def gain_columns(flat, out):
    rows = flat[pl.ds(0, 16, stride=4 * A_ROWS), :]
    r = lax.broadcasted_iota(jnp.int32, (D, 16), 0) // 9
    spread = dot((r == lax.broadcasted_iota(jnp.int32, (D, 16), 1)).astype(f32), rows)
    lane = lax.broadcasted_iota(jnp.int32, (D, 128), 1)
    e = lax.rem(lax.broadcasted_iota(jnp.int32, (D, 128), 0), 9)
    for i in (0, 1):
        out[:, i : i + 1] = jnp.sum(jnp.where(lane == e + 108 + 9 * i, spread, 0.0), axis=1, keepdims=True)


def gain_rows(partial, flat):
    pos = lax.broadcasted_iota(jnp.int32, (128, D), 0)
    r = lax.broadcasted_iota(jnp.int32, (128, D), 1) // 9
    pick = (lax.rem(pos, 64) // 4 == r).astype(f32)
    lane = lax.broadcasted_iota(jnp.int32, (D, 128), 1)
    e = lax.rem(lax.broadcasted_iota(jnp.int32, (D, 128), 0), 9)
    cols = jnp.zeros((D, 128), f32)
    for i in (0, 1):
        cols += jnp.where(lane == e + 108 + 9 * i, jnp.sum(partial[i], axis=1, keepdims=True), 0.0)
    spread = dot(pick, cols, precision=lax.Precision.HIGHEST)
    flat[pl.ds(0, 128, stride=A_ROWS), :] += spread


def series_scalars(targets, lag_mask, date_mask, freq, sets, factor, stats):
    scale = jnp.sum(jnp.abs(targets[...]), axis=1, keepdims=True) / LEN + 1e-5
    lag = lag_mask[...].astype(f32) / scale
    second = lax.broadcasted_iota(jnp.int32, (2, NDATE), 0) == 1
    start = jnp.where(second, freq[1], freq[0]) * (NDATE // 3)
    keep = jnp.where(lax.broadcasted_iota(jnp.int32, (2, NDATE), 1) >= start, date_mask[...], 0).astype(f32)
    both = jnp.concatenate([lag, keep], axis=1)
    both = jnp.concatenate([both, jnp.zeros((2, 32), f32)], axis=1)
    both = jnp.concatenate([both, jnp.zeros((6, 128), f32)], axis=0)
    factor[...] = both.T
    lane = lax.broadcasted_iota(jnp.int32, (1, 128), 1)
    row = jnp.zeros((1, 128), f32)
    for s in (0, 1):
        row += jnp.where(lane == sets[s], scale[s : s + 1], 0.0) + jnp.where(lane == sets[s] + NSET, 1.0, 0.0)
    stats[...] = row

def fold(op, a):
    return op(a.reshape(a.shape[0] // 8, 8, a.shape[1]), axis=0)


def weave(gens):
    gens = list(gens)
    while gens:
        for g in list(gens):
            try:
                next(g)
            except StopIteration:
                gens.remove(g)


VM = pl.BlockSpec(memory_space=pltpu.VMEM)
SM = pl.BlockSpec(memory_space=pltpu.SMEM)
HB = pl.BlockSpec(memory_space=pl.ANY)
NAMES = ("in", "qkv", "out", "gu", "down")


def tiled(name):
    return (-(-SPECS[name][0] // 128), ROWS[name], 128)


def attend(s, hh, q, k, v, prob, sbuf, rl, osum, mixed):
    diag = lambda c0: (lax.broadcasted_iota(jnp.int32, (CH, QT), 0) + c0) <= lax.broadcasted_iota(jnp.int32, (CH, QT), 1)
    heads = [hh * GROUP + u for u in range(GROUP)]
    kts = [k[s, h].astype(f32).T.astype(bf16) for h in heads]
    ones = (lax.broadcasted_iota(jnp.int32, (HD, LEN), 0) == 0).astype(f32).astype(bf16)
    vs = [jnp.concatenate([v[s, h], ones], axis=0) for h in heads]
    tasks = [(u, j) for j in range(LEN // QT - 1, -1, -1) for u in range(GROUP)]
    tops = {}

    def score(i):
        u, j = tasks[i]
        n, best = (j + 1) * QT, None
        for c in range(0, n, CH):
            x = dot(kts[u][c : c + CH], q[s, heads[u], :, j * QT : j * QT + QT])
            if c + CH > n - QT:
                x = jnp.where(diag(c - (n - QT)), x, -1e30)
            sbuf[i % 2, c : c + CH] = x
            top = fold(jnp.max, x)
            best = top if best is None else jnp.maximum(best, top)
            yield
        tops[i] = jnp.max(best, axis=0, keepdims=True)

    def exponent(i):
        u, j = tasks[i]
        for c in range(0, (j + 1) * QT, CH):
            prob[j][s, heads[u], c : c + CH] = jnp.exp(sbuf[i % 2, c : c + CH] - tops[i]).astype(bf16)
            yield

    def mix(i):
        u, j = tasks[i]
        h, n, cols = heads[u], (j + 1) * QT, pl.ds(j * QT, QT)
        o = dot(vs[u][:, :n], prob[j][s, h])
        inv = 1.0 / o[HD : HD + 1]
        o = o[:HD] * inv
        rl[s, h, :, cols] = inv
        osum[s, h, :, cols] = o
        mixed[s, h, :, cols] = o.astype(bf16)

    last = len(tasks)
    for i in range(last + 3):
        if 0 <= i - 3:
            mix(i - 3)
        weave(([score(i)] if i < last else []) + ([exponent(i - 1)] if 0 <= i - 1 < last else []))


def attend_back(s, hh, q, k, v, prob, rl, osum, gmixed, cosr, sinr, gjoint, dsb, dq, dk, dv):
    heads = [hh * GROUP + u for u in range(GROUP)]
    dos, deltas, vts = [], [], []
    for h in heads:
        do = (gmixed[s, h] * rl[s, h]).astype(bf16)
        dos.append(do)
        deltas.append(jnp.sum(do.astype(f32) * osum[s, h], axis=0, keepdims=True))
        vts.append(v[s, h].astype(f32).T.astype(bf16))
    dk[...] = jnp.zeros_like(dk)
    dv[...] = jnp.zeros_like(dv)
    tasks = [(u, j) for j in range(LEN // QT - 1, -1, -1) for u in range(GROUP)]

    def spread(i):
        u, j = tasks[i]
        n = (j + 1) * QT
        cols = slice(j * QT, n)
        for c in range(0, n, QT):
            dp = dot(vts[u][c : c + QT], dos[u][:, cols]) - deltas[u][:, cols]
            dsb[i % 2, c : c + QT] = (prob[j][s, heads[u], c : c + QT].astype(f32) * dp).astype(bf16)
            yield

    def to_query(i):
        u, j = tasks[i]
        n = (j + 1) * QT
        dq[u, :, j * QT : n] = dot(k[s, heads[u]][:, :n], dsb[i % 2, :n])
        yield

    def to_keys(i):
        u, j = tasks[i]
        for c in range(0, (j + 1) * QT, QT):
            dk[u, :, c : c + QT] += dot(q[s, heads[u], :, j * QT : j * QT + QT], dsb[i % 2, c : c + QT], 1, 1)
            yield

    def to_values(i):
        u, j = tasks[i]
        for c in range(0, (j + 1) * QT, QT):
            dv[u, :, c : c + QT] += dot(dos[u][:, j * QT : j * QT + QT], prob[j][s, heads[u], c : c + QT], 1, 1)
            yield

    last = len(tasks)
    for i in range(last + 1):
        weave(([spread(i)] if i < last else []) + ([to_query(i - 1), to_keys(i - 1), to_values(i - 1)] if i else []))
    c, sn = cosr[...], sinr[...]
    for u, h in enumerate(heads):
        for which, val in ((0, dq[u] * 0.25), (1, dk[u])):
            a, b = val[:8], val[8:]
            gjoint[s, which, h] = jnp.concatenate([a * c + b * sn, b * c - a * sn], axis=0).astype(bf16)
        gjoint[s, 2, h] = dv[u].astype(bf16)


def layer_kernel(
    feats_h, targets_h, lag_h, date_h, freq_h, sets_h, w_in_h, w_qkv_h, w_out_h, w_gu_h, w_down_h, gains_h, dout_h, cos_h, sin_h,
    out_h, gfeats_h, tot_a, tot_b,
    feats, dout, targets, lag_mask, date_mask, freq, sets, w_in, w_qkv, w_out, w_gu, w_down, gains_own, cosr, sinr, out, gfeats,
    tile_a, tile_b, all_a, all_b, flat_a, flat_b, half_a, half_b, row_a, row_b, line_b,
    m_in, m_qkv, m_out, m_gu, m_down, win, wqkv, wout, wgu, wdown, winT, wqkvT, woutT, wguT, wdownT,
    gains, g_gain, factor, stats, lifted, first, inv1, normed, q, k, v, p0, p1, p2, p3, sbuf, rl, osum, mixed, middle, second, hidden, both,
    gmid, gbranch, gmixed, gjoint, gfirst, dsb, dq, dk, dv, sem_a, sem_b, sem_c, sem_d, sem_l, sem_x, sem_z,
):
    knock()
    prob = (p0, p1, p2, p3)
    loads = [
        pltpu.make_async_copy(src, dst, sem_l.at[i])
        for i, (src, dst) in enumerate(
            (
                (w_in_h, w_in), (w_qkv_h, w_qkv), (w_out_h, w_out), (w_gu_h, w_gu), (w_down_h, w_down), (gains_h, gains_own),
                (feats_h, feats), (targets_h, targets), (lag_h, lag_mask), (date_h, date_mask), (freq_h, freq), (sets_h, sets),
                (cos_h, cosr), (sin_h, sinr), (dout_h, dout),
            )
        )
    ]
    for load in loads:
        load.start()
    for load in loads[:6]:
        load.wait()
    own_tiles(w_in, w_qkv, w_out, w_gu, w_down, gains_own, tile_a, tile_b, flat_b.at[pl.ds(0, B_ROWS)])
    a, b = GatherDirect(tile_a, all_a, sem_a), Gather(tile_b, all_b, sem_b)

    def scalars():
        for load in loads[7:12]:
            load.wait()
        series_scalars(targets, lag_mask, date_mask, freq, sets, factor, stats)
        g_gain[...] = jnp.zeros_like(g_gain)

    def lift():
        for load in loads[6:7] + loads[12:14]:
            load.wait()
        for s in (0, 1):
            lifted[s] = (feats[s].astype(f32) * factor[:F, s : s + 1]).astype(bf16)

    enter(sem_x, sem_z, a.to, (scalars, lift))
    a.second()
    b.first()
    a.last()
    flat_a[...] = all_a[...].reshape(128 * A_ROWS, 128)
    gain_columns(flat_a, gains)

    def emit(name, flat, rows, mat, out, outT):
        unpack(flat, rows, name, mat)
        for t, at, width in lane_tiles(SPECS[name][0]):
            val = mat[t][:, :width]
            out[:, at : at + width] = val.astype(bf16)
            outT[at : at + width, :] = val.T.astype(bf16)
        mat[...] = jnp.zeros_like(mat)

    emit("in", flat_a, A_ROWS, m_in, win, winT)
    emit("qkv", flat_a, A_ROWS, m_qkv, wqkv, wqkvT)

    def add_to(ref, val):
        for t, at, width in lane_tiles(val.shape[1]):
            ref[t, :, :width] += val[:, at : at + width]

    gain0 = gains[:, 0:1]
    gain1 = gains[:, 1:2]

    @pl.loop(0, 2)
    def _(s):
        @pl.loop(0, LEN // TOK_IN)
        def _(i):
            t = pl.ds(pl.multiple_of(i * TOK_IN, TOK_IN), TOK_IN)
            x = dot(winT[...], lifted[s, :, t])
            first[s, :, t] = x
            r = lax.rsqrt(jnp.mean(x * x, axis=0, keepdims=True) + EPS)
            inv1[s, :, t] = r
            n = (x * r * gain0).astype(bf16)
            normed[s, :, t] = n
            joint = dot(wqkvT[...], n).reshape(3, H, HD, TOK_IN)
            c, sn = cosr[:, t][None], sinr[:, t][None]
            for which, ref, scale in ((0, q, 0.25), (1, k, 1.0)):
                u, w = joint[which, :, :8], joint[which, :, 8:]
                ref[s, :, :, t] = (jnp.concatenate([u * c - w * sn, w * c + u * sn], axis=1) * scale).astype(bf16)
            v[s, :, :, t] = joint[2].astype(bf16)

    b.second()

    @pl.loop(0, 2)
    def _(s):
        @pl.loop(0, H // GROUP)
        def _(hh):
            attend(s, hh, q, k, v, prob, sbuf, rl, osum, mixed)

        @pl.when(s == 0)
        def _():
            b.third()

    b.last()
    flat_b[...] = all_b[...].astype(f32).reshape(128 * B_ROWS, 128)
    emit("out", flat_b, B_ROWS, m_out, wout, woutT)
    emit("gu", flat_b, B_ROWS, m_gu, wgu, wguT)
    emit("down", flat_b, B_ROWS, m_down, wdown, wdownT)
    loads[14].wait()

    @pl.loop(0, 2)
    def _(s):
        @pl.loop(0, LEN // TOK_MLP)
        def _(i):
            t = pl.ds(pl.multiple_of(i * TOK_MLP, TOK_MLP), TOK_MLP)
            mid = first[s, :, t] + dot(woutT[...], mixed[s, :, :, t].reshape(D, TOK_MLP))
            r = lax.rsqrt(jnp.mean(mid * mid, axis=0, keepdims=True) + EPS)
            sec = (mid * r * gain1).astype(bf16)
            second[:, t] = sec
            g = dout[s, :, t]
            for f in range(0, FF, 128):
                gate = dot(wguT[f : f + 128], sec)
                up = dot(wguT[FF + f : FF + f + 128], sec)
                gh = dot(wdown[f : f + 128], g)
                sig = 1.0 / (1.0 + jnp.exp(-gate))
                silu = gate * sig
                hidden[s, f : f + 128, t] = (silu * up).astype(bf16)
                both[FF + f : FF + f + 128, t] = (gh * silu).astype(bf16)
                both[f : f + 128, t] = (gh * up * (sig + silu * (1.0 - sig))).astype(bf16)
            middle[s, :, t] = mid
            c = dot(wgu[...], both[:, t])
            cg = c * gain1
            inner = jnp.mean(cg * mid, axis=0, keepdims=True)
            gain_part = c * mid * r
            g_gain[1] += functools.reduce(jnp.add, [gain_part[:, x : x + 128] for x in range(0, TOK_MLP, 128)])
            gm = g.astype(f32) + r * cg - mid * (r * r * r * inner)
            gmid[s, :, t] = gm
            gb = gm.astype(bf16)
            gbranch[:, t] = gb
            gmixed[s, :, :, t] = dot(wout[...], gb).reshape(H, HD, TOK_MLP)

        add_to(m_down, dot(hidden[s], dout[s], 1, 1))
        add_to(m_gu, dot(second[...], both[...], 1, 1))
        add_to(m_out, dot(mixed[s].reshape(D, LEN), gbranch[...], 1, 1))

    flat_b[...] = jnp.zeros_like(flat_b)
    pack(m_out, "out", flat_b, B_ROWS)
    pack(m_gu, "gu", flat_b, B_ROWS)
    pack(m_down, "down", flat_b, B_ROWS)
    all_b[...] = flat_b[...].reshape(all_b.shape).astype(bf16)
    a, b = ReduceDirect(all_a, half_a, row_a, sem_c), Reduce(all_b, half_b, row_b, line_b, sem_d)
    b.first()

    @pl.loop(0, 2)
    def _(s):
        @pl.loop(0, H // GROUP)
        def _(hh):
            attend_back(s, hh, q, k, v, prob, rl, osum, gmixed, cosr, sinr, gjoint, dsb, dq, dk, dv)

        @pl.when(s == 0)
        def _():
            b.second()

    b.third()

    @pl.loop(0, 2)
    def _(s):
        add_to(m_qkv, dot(normed[s], gjoint[s].reshape(3 * D, LEN), 1, 1))
        @pl.loop(0, LEN // TOK_BACK)
        def _(i):
            t = pl.ds(pl.multiple_of(i * TOK_BACK, TOK_BACK), TOK_BACK)
            c = dot(wqkv[...], gjoint[s, :, :, :, t].reshape(3 * D, TOK_BACK))
            x, r = first[s, :, t], inv1[s, :, t]
            cg = c * gain0
            inner = jnp.mean(cg * x, axis=0, keepdims=True)
            gain_part = c * x * r
            g_gain[0] += functools.reduce(jnp.add, [gain_part[:, x : x + 128] for x in range(0, TOK_BACK, 128)])
            gf = (gmid[s, :, t] + r * cg - x * (r * r * r * inner)).astype(bf16)
            gfirst[s, :, t] = gf

        add_to(m_in, dot(lifted[s], gfirst[s], 1, 1))

    flat_a[...] = jnp.zeros_like(flat_a)
    pack(m_in, "in", flat_a, A_ROWS)
    pack(m_qkv, "qkv", flat_a, A_ROWS)
    gain_rows(g_gain, flat_a)
    flat_a[pl.ds(5, 128, stride=A_ROWS), :] = jnp.broadcast_to(stats[...], (128, 128))
    all_a[...] = flat_a[...].reshape(all_a.shape)
    a.first()
    tot_b[...] = b.last()
    a.second()

    for s in (0, 1):
        out[s] = (middle[s] + dot(wdownT[...], hidden[s])).astype(bf16)
        gfeats[s] = (dot(win[...], gfirst[s]) * factor[:F, s : s + 1]).astype(bf16)
    store_out = pltpu.make_async_copy(out, out_h, sem_l.at[15])
    store_out.start()
    store_gfeats = pltpu.make_async_copy(gfeats, gfeats_h, sem_l.at[16])
    store_gfeats.start()
    tot_a[...] = a.last()
    store_out.wait()
    store_gfeats.wait()


def run_layer(feats_t, targets, lag_mask, date_mask, freq_ids, dataset_ids, weights, gains, dout_t):
    cos, sin = rope_tables()
    sd, V = jax.ShapeDtypeStruct, pltpu.VMEM
    shapes = [(ROWS[n], SPECS[n][0]) for n in NAMES]
    return pl.pallas_call(
        layer_kernel,
        in_specs=[HB] * 15,
        out_specs=[HB, HB, VM, VM],
        out_shape=[sd((2, D, LEN), bf16), sd((2, F, LEN), bf16), sd((A_ROWS, 128), f32), sd((B_ROWS, 128), f32)],
        scratch_shapes=[
            V((2, F, LEN), bf16), V((2, D, LEN), bf16), V((2, LEN), f32), V((2, NLAG), jnp.int32), V((2, NDATE), jnp.int32),
            *[pltpu.SMEM((2,), jnp.int32)] * 2,
            *[V((SPECS[n][1],), bf16) for n in NAMES], V((2, 9), bf16), V((8, LEN), f32), V((8, LEN), f32),
            V((2, D, LEN), bf16), V((2, F, LEN), bf16),
            V((A_ROWS, 128), f32), V((B_ROWS, 128), bf16),
            V((2, 64, A_ROWS, 128), f32), V((2, 16, 4, B_ROWS, 128), bf16),
            V((128 * A_ROWS, 128), f32), V((128 * B_ROWS, 128), f32),
            V((64, A_ROWS, 128), f32), V((16, 4, B_ROWS, 128), bf16),
            V((64, A_ROWS, 128), f32), V((16, 4, B_ROWS, 128), bf16),
            V((4, B_ROWS, 128), bf16),
            *[V(tiled(n), f32) for n in NAMES], *[V(s, bf16) for s in shapes], *[V(s[::-1], bf16) for s in shapes],
            V((D, 2), f32), V((2, D, 128), f32), V((128, 8), f32), V((1, 128), f32),
            V((2, F, LEN), bf16), V((2, D, LEN), f32), V((2, 1, LEN), f32), V((2, D, LEN), bf16),
            V((2, H, HD, LEN), bf16), V((2, H, HD, LEN), bf16), V((2, H, HD, LEN), bf16),
            *[V((2, H, (j + 1) * QT, QT), bf16) for j in range(4)],
            V((2, LEN, QT), f32), V((2, H, 1, LEN), f32), V((2, H, HD, LEN), f32), V((2, H, HD, LEN), bf16),
            V((2, D, LEN), f32), V((D, LEN), bf16), V((2, FF, LEN), bf16), V((2 * FF, LEN), bf16),
            V((2, D, LEN), f32), V((D, LEN), bf16), V((2, H, HD, LEN), f32), V((2, 3, H, HD, LEN), bf16), V((2, D, LEN), bf16),
            V((2, LEN, QT), bf16), *[V((GROUP, HD, LEN), f32)] * 3,
            *[pltpu.SemaphoreType.DMA((2, 3))] * 4, pltpu.SemaphoreType.DMA((17,)), *[pltpu.SemaphoreType.REGULAR] * 2,
        ],
        compiler_params=pltpu.CompilerParams(collective_id=0, has_side_effects=True, vmem_limit_bytes=63 * 2**20),
    )(feats_t, targets, lag_mask, date_mask, freq_ids, dataset_ids, *weights, gains, dout_t, jnp.asarray(cos), jnp.asarray(sin))


def finish_kernel(out_h, gfeats_h, tot_a_h, tot_b_h, running_h, out, gfeats, o_in, o_qkv, o_out, o_gu, o_down, o_gain, o_running,
                  out_v, gfeats_v, tot_a, tot_b, running, sems):
    pairs = ((tot_a_h, tot_a), (tot_b_h, tot_b), (running_h, running), (out_h, out_v), (gfeats_h, gfeats_v))
    copies = [pltpu.make_async_copy(src, dst, sems.at[i]) for i, (src, dst) in enumerate(pairs)]
    stores = [pltpu.make_async_copy(src, dst, sems.at[5 + i]) for i, (src, dst) in enumerate(((out_v, out), (gfeats_v, gfeats)))]
    for copy in copies:
        copy.start()
    for copy in copies:
        copy.wait()
    for store in stores:
        store.start()
    for name, ref in (("in", o_in), ("qkv", o_qkv), ("out", o_out), ("gu", o_gu), ("down", o_down)):
        _, chunk, _, _, which, base = SPECS[name]
        for t, at, width in lane_tiles(chunk):
            ref[pl.ds(at, width)] = (tot_a if which == "a" else tot_b)[base + t, :width]
    o_gain[0:1, :] = tot_a[0:1, 108:117]
    o_gain[1:2, :] = tot_a[0:1, 117:126]
    sums, counts = tot_a[5, :NSET], tot_a[5, NSET : 2 * NSET]
    old = running[...]
    o_running[...] = jnp.where(counts > 0.5, 0.75 * old + 0.25 * (sums / jnp.maximum(counts, 1.0)), old)
    for store in stores:
        store.wait()


def hand_out(out, gfeats, tot_a, tot_b, running):
    sd, V = jax.ShapeDtypeStruct, pltpu.VMEM
    return pl.pallas_call(
        finish_kernel,
        in_specs=[HB] * 5,
        out_specs=[HB, HB] + [VM] * 7,
        out_shape=[sd((2, D, LEN), bf16), sd((2, F, LEN), bf16)]
        + [sd((SPECS[n][1],), f32) for n in NAMES] + [sd((2, 9), f32), sd((NSET,), f32)],
        scratch_shapes=[V((2, D, LEN), bf16), V((2, F, LEN), bf16), V((A_ROWS, 128), f32), V((B_ROWS, 128), f32), V((NSET,), f32),
                        pltpu.SemaphoreType.DMA((7,))],
        compiler_params=pltpu.CompilerParams(vmem_limit_bytes=60 * 2**20),
    )(out, gfeats, tot_a, tot_b, running)


def body(feats, targets, lag_mask, date_mask, freq_ids, dataset_ids, w_in, w_qkv, w_out, w_gu, w_down, gains, running, d_out):
    done = run_layer(
        jnp.swapaxes(feats, 1, 2), targets, lag_mask, date_mask, freq_ids, dataset_ids,
        (w_in, w_qkv, w_out, w_gu, w_down), gains, jnp.swapaxes(d_out, 1, 2),
    )
    out, gfeats, *rest = hand_out(*done, running)
    return (jnp.swapaxes(out, 1, 2), jnp.swapaxes(gfeats, 1, 2), *rest)


def solution(mesh):
    flat, rows, cube = P(BOTH), P(BOTH, None), P(BOTH, None, None)
    return jax.shard_map(
        body,
        mesh=mesh,
        in_specs=(cube, rows, rows, rows, flat, flat, flat, flat, flat, flat, flat, P(None, "dp"), P(), cube),
        out_specs=(cube, cube, flat, flat, flat, flat, flat, P(None, "dp"), P()),
        check_vma=False,
    )
```

profile of v0, /device:TPU:1, one launch (start us, length us, event | category | flops | bytes accessed | tf_op | source)
XLA Modules:
  0.0 79.7 jit_solution(16716986423811144674)
XLA Ops:
  0.6 76.2 %shard_map.223 = (bf16[2,144,1024]{2,1,0:T(8,128)(2,1)}, bf16[2,96,1024]{2,1,0:T(8,128)(2,1)}, f32[8,128]{1,0:T(8,128)}, f32[16,128]{1,0:T(8,128)}) custom-call(bf16[2,96,1024]{2,1,0:T(8,128)(2,1)} %bitcast.5, f32[2,1024]{1,0:T(2,128)} %targets_h.1, s32[2,84]{1,0:T(2,128)} %lag_h.1, s32[2,12]{1,0:T(2,128)} %date_h.1, s32[2]{0:T(128)} %freq_h.1, s32[2]{0:T(128)} %sets_h.1, ...), custom_call_target="tpu_custom_call" | custom-call | tf_op jit(solution)/shard_map/pallas_call | solution.py:659
  76.9 2.8 %shard_map.224 = (bf16[2,144,1024]{2,1,0:T(8,128)(2,1)}, bf16[2,96,1024]{2,1,0:T(8,128)(2,1)}, f32[108]{0:T(128)}, f32[486]{0:T(512)}, f32[162]{0:T(256)}, /*ind...) custom-call(bf16[2,144,1024]{2,1,0:T(8,128)(2,1)} %get-tuple-element.22.out_h, ...), custom_call_target="tpu_custom_call" | custom-call | tf_op jit(solution)/shard_map/pallas_call | solution.py:716
where the time goes:
time: 79.9 us; the launch traced here: 79.7 us
  Pallas kernels  79 us (99%)
    pallas_call x1, Pallas kernels, run_layer(): pl.pallas_call(layer_kernel, in_specs=[HB] * 15, out_specs=[HB, HB, VM, V...  76.2 us
    pallas_call x1, Pallas kernels, hand_out(): pl.pallas_call(finish_kernel, in_specs=[HB] * 5, out_specs=[HB, HB] + [VM...  2.81 us

commit v1 on v0

--- a/solution.py
+++ b/solution.py
@@ -13,7 +13,7 @@
 TOK_IN = 1024
 TOK_MLP = 1024
 TOK_BACK = 1024
-QT = 256
+BLOCK = 128
 CH = 128
 GROUP = 3
 f32, bf16 = jnp.float32, jnp.bfloat16
@@ -137,15 +137,16 @@
     pl.semaphore_wait(pltpu.get_barrier_semaphore(), 10)
     for o in STEPS:
         signal(sem_x, device(0, o, 0))
+    work[0]()
     for line in LINES:
         send_to(*line)
-    work[0]()
+    work[1]()
     pl.semaphore_wait(sem_x, 3)
     for o in STEPS:
         signal(sem_z, device(o, 0, 0))
     for line in X_PLANES:
         send_to(*line)
-    work[1]()
+    work[2]()
     pl.semaphore_wait(sem_z, 3)
     for line in REST:
         send_to(*line)
@@ -173,12 +174,12 @@
         dp, y, core = place()
         self.all[core, 4 * dp + y] = self.own[...]
         wait(self.all.at[core, pl.ds(0, 63)], self.sems.at[1, 0])
-        wait(self.all.at[core, pl.ds(0, 63)], self.sems.at[0, 0])
         send(self.all.at[core], self.all.at[core], self.sems, 1, partners()[2])
 
     def last(self):
         _, _, core = place()
         wait(self.all.at[core], self.sems.at[1, 1])
+        wait(self.all.at[core, pl.ds(0, 63)], self.sems.at[0, 0])
         wait(self.all.at[core], self.sems.at[0, 1])
 
 
@@ -361,22 +362,41 @@
     return (-(-SPECS[name][0] // 128), ROWS[name], 128)
 
 
-def attend(s, hh, q, k, v, prob, sbuf, rl, osum, mixed):
-    diag = lambda c0: (lax.broadcasted_iota(jnp.int32, (CH, QT), 0) + c0) <= lax.broadcasted_iota(jnp.int32, (CH, QT), 1)
-    heads = [hh * GROUP + u for u in range(GROUP)]
-    kts = [k[s, h].astype(f32).T.astype(bf16) for h in heads]
+def heads_of(hh):
+    return [hh * GROUP + u for u in range(GROUP)]
+
+
+TASKS = [(u, j) for j in range(LEN // BLOCK - 1, -1, -1) for u in range(GROUP)]
+
+
+def chunks(n, size):
+    return [(c, min(size, n - c)) for c in range(0, n, size)]
+
+
+def corners(pair, cols):
+    empty = jnp.zeros((HD, BLOCK), bf16)
+    return jnp.concatenate(
+        [jnp.concatenate([pair[0][:, cols], empty], axis=1), jnp.concatenate([empty, pair[1][:, cols]], axis=1)], axis=0
+    )
+
+
+def attend(hh, q, k, v, prob, sbuf, rl, osum, mixed):
+    heads = heads_of(hh)
+    kts = [jnp.concatenate([k[0, h], k[1, h]], axis=0).astype(f32).T.astype(bf16) for h in heads]
     ones = (lax.broadcasted_iota(jnp.int32, (HD, LEN), 0) == 0).astype(f32).astype(bf16)
-    vs = [jnp.concatenate([v[s, h], ones], axis=0) for h in heads]
-    tasks = [(u, j) for j in range(LEN // QT - 1, -1, -1) for u in range(GROUP)]
+    vs = [jnp.concatenate([v[0, h], v[1, h], ones], axis=0) for h in heads]
+    row = lax.broadcasted_iota(jnp.int32, (BLOCK, 2 * BLOCK), 0)
+    diagonal = row <= lax.rem(lax.broadcasted_iota(jnp.int32, (BLOCK, 2 * BLOCK), 1), BLOCK)
     tops = {}
 
     def score(i):
-        u, j = tasks[i]
-        n, best = (j + 1) * QT, None
+        u, j = TASKS[i]
+        n, best = (j + 1) * BLOCK, None
+        both = corners((q[0, heads[u]], q[1, heads[u]]), slice(j * BLOCK, n))
         for c in range(0, n, CH):
-            x = dot(kts[u][c : c + CH], q[s, heads[u], :, j * QT : j * QT + QT])
-            if c + CH > n - QT:
-                x = jnp.where(diag(c - (n - QT)), x, -1e30)
+            x = dot(kts[u][c : c + CH], both)
+            if c + CH == n:
+                x = jnp.where(diagonal, x, -1e30)
             sbuf[i % 2, c : c + CH] = x
             top = fold(jnp.max, x)
             best = top if best is None else jnp.maximum(best, top)
@@ -384,76 +404,91 @@
         tops[i] = jnp.max(best, axis=0, keepdims=True)
 
     def exponent(i):
-        u, j = tasks[i]
-        for c in range(0, (j + 1) * QT, CH):
-            prob[j][s, heads[u], c : c + CH] = jnp.exp(sbuf[i % 2, c : c + CH] - tops[i]).astype(bf16)
+        u, j = TASKS[i]
+        for c in range(0, (j + 1) * BLOCK, CH):
+            prob[j][heads[u], c : c + CH] = jnp.exp(sbuf[i % 2, c : c + CH] - tops[i]).astype(bf16)
             yield
 
     def mix(i):
-        u, j = tasks[i]
-        h, n, cols = heads[u], (j + 1) * QT, pl.ds(j * QT, QT)
-        o = dot(vs[u][:, :n], prob[j][s, h])
-        inv = 1.0 / o[HD : HD + 1]
-        o = o[:HD] * inv
-        rl[s, h, :, cols] = inv
-        osum[s, h, :, cols] = o
-        mixed[s, h, :, cols] = o.astype(bf16)
-
-    last = len(tasks)
+        u, j = TASKS[i]
+        h, n, cols = heads[u], (j + 1) * BLOCK, pl.ds(j * BLOCK, BLOCK)
+        o = None
+        for c, w in chunks(n, 2 * BLOCK):
+            x = dot(vs[u][:, c : c + w], prob[j][h, c : c + w])
+            o = x if o is None else o + x
+            yield
+        inv = 1.0 / o[2 * HD : 2 * HD + 1]
+        for s in (0, 1):
+            part = slice(s * BLOCK, s * BLOCK + BLOCK)
+            own = o[s * HD : s * HD + HD, part] * inv[:, part]
+            rl[s, h, :, cols] = inv[:, part]
+            osum[s, h, :, cols] = own
+            mixed[s, h, :, cols] = own.astype(bf16)
+
+    last = len(TASKS)
     for i in range(last + 3):
-        if 0 <= i - 3:
-            mix(i - 3)
-        weave(([score(i)] if i < last else []) + ([exponent(i - 1)] if 0 <= i - 1 < last else []))
-
-
-def attend_back(s, hh, q, k, v, prob, rl, osum, gmixed, cosr, sinr, gjoint, dsb, dq, dk, dv):
-    heads = [hh * GROUP + u for u in range(GROUP)]
-    dos, deltas, vts = [], [], []
+        weave(
+            ([mix(i - 3)] if 0 <= i - 3 else [])
+            + ([score(i)] if i < last else [])
+            + ([exponent(i - 1)] if 0 <= i - 1 < last else [])
+        )
+
+
+def attend_back(hh, q, k, v, prob, rl, osum, gmixed, cosr, sinr, gjoint, dsb, dq, dk, dv):
+    heads = heads_of(hh)
+    dos, deltas, vts, ks = [], [], [], []
     for h in heads:
-        do = (gmixed[s, h] * rl[s, h]).astype(bf16)
-        dos.append(do)
-        deltas.append(jnp.sum(do.astype(f32) * osum[s, h], axis=0, keepdims=True))
-        vts.append(v[s, h].astype(f32).T.astype(bf16))
+        pair = [(gmixed[s, h] * rl[s, h]).astype(bf16) for s in (0, 1)]
+        dos.append(pair)
+        deltas.append([jnp.sum(pair[s].astype(f32) * osum[s, h], axis=0, keepdims=True) for s in (0, 1)])
+        vts.append(jnp.concatenate([v[0, h], v[1, h]], axis=0).astype(f32).T.astype(bf16))
+        ks.append(jnp.concatenate([k[0, h], k[1, h]], axis=0))
     dk[...] = jnp.zeros_like(dk)
     dv[...] = jnp.zeros_like(dv)
-    tasks = [(u, j) for j in range(LEN // QT - 1, -1, -1) for u in range(GROUP)]
 
     def spread(i):
-        u, j = tasks[i]
-        n = (j + 1) * QT
-        cols = slice(j * QT, n)
-        for c in range(0, n, QT):
-            dp = dot(vts[u][c : c + QT], dos[u][:, cols]) - deltas[u][:, cols]
-            dsb[i % 2, c : c + QT] = (prob[j][s, heads[u], c : c + QT].astype(f32) * dp).astype(bf16)
+        u, j = TASKS[i]
+        n = (j + 1) * BLOCK
+        cols = slice(j * BLOCK, n)
+        both = corners(dos[u], cols)
+        delta = jnp.concatenate([deltas[u][0][:, cols], deltas[u][1][:, cols]], axis=1)
+        for c, w in chunks(n, 2 * BLOCK):
+            dp = dot(vts[u][c : c + w], both) - delta
+            dsb[i % 2, c : c + w] = (prob[j][heads[u], c : c + w].astype(f32) * dp).astype(bf16)
             yield
 
     def to_query(i):
-        u, j = tasks[i]
-        n = (j + 1) * QT
-        dq[u, :, j * QT : n] = dot(k[s, heads[u]][:, :n], dsb[i % 2, :n])
+        u, j = TASKS[i]
+        n = (j + 1) * BLOCK
+        x = dot(ks[u][:, :n], dsb[i % 2, :n])
+        for s in (0, 1):
+            dq[u, s, :, j * BLOCK : n] = x[s * HD : s * HD + HD, s * BLOCK : s * BLOCK + BLOCK]
         yield
 
     def to_keys(i):
-        u, j = tasks[i]
-        for c in range(0, (j + 1) * QT, QT):
-            dk[u, :, c : c + QT] += dot(q[s, heads[u], :, j * QT : j * QT + QT], dsb[i % 2, c : c + QT], 1, 1)
+        u, j = TASKS[i]
+        both = corners((q[0, heads[u]], q[1, heads[u]]), slice(j * BLOCK, (j + 1) * BLOCK))
+        for c, w in chunks((j + 1) * BLOCK, 2 * BLOCK):
+            dk[u, :, c : c + w] += dot(both, dsb[i % 2, c : c + w], 1, 1)
             yield
 
     def to_values(i):
-        u, j = tasks[i]
-        for c in range(0, (j + 1) * QT, QT):
-            dv[u, :, c : c + QT] += dot(dos[u][:, j * QT : j * QT + QT], prob[j][s, heads[u], c : c + QT], 1, 1)
+        u, j = TASKS[i]
+        both = corners(dos[u], slice(j * BLOCK, (j + 1) * BLOCK))
+        for c, w in chunks((j + 1) * BLOCK, 2 * BLOCK):
+            dv[u, :, c : c + w] += dot(both, prob[j][heads[u], c : c + w], 1, 1)
             yield
 
-    last = len(tasks)
+    last = len(TASKS)
     for i in range(last + 1):
-        weave(([spread(i)] if i < last else []) + ([to_query(i - 1), to_keys(i - 1), to_values(i - 1)] if i else []))
+        weave(([spread(i), to_values(i)] if i < last else []) + ([to_keys(i - 1), to_query(i - 1)] if i else []))
     c, sn = cosr[...], sinr[...]
     for u, h in enumerate(heads):
-        for which, val in ((0, dq[u] * 0.25), (1, dk[u])):
-            a, b = val[:8], val[8:]
-            gjoint[s, which, h] = jnp.concatenate([a * c + b * sn, b * c - a * sn], axis=0).astype(bf16)
-        gjoint[s, 2, h] = dv[u].astype(bf16)
+        for s in (0, 1):
+            for which, val in ((0, dq[u, s] * 0.25), (1, dk[u, s * HD : s * HD + HD])):
+                a, b = val[:8], val[8:]
+                gjoint[s, which, h] = jnp.concatenate([a * c + b * sn, b * c - a * sn], axis=0).astype(bf16)
+            gjoint[s, 2, h] = dv[u, s * HD : s * HD + HD].astype(bf16)
 
 
 def layer_kernel(
@@ -462,11 +497,13 @@
     feats, dout, targets, lag_mask, date_mask, freq, sets, w_in, w_qkv, w_out, w_gu, w_down, gains_own, cosr, sinr, out, gfeats,
     tile_a, tile_b, all_a, all_b, flat_a, flat_b, half_a, half_b, row_a, row_b, line_b,
     m_in, m_qkv, m_out, m_gu, m_down, win, wqkv, wout, wgu, wdown, winT, wqkvT, woutT, wguT, wdownT,
-    gains, g_gain, factor, stats, lifted, first, inv1, normed, q, k, v, p0, p1, p2, p3, sbuf, rl, osum, mixed, middle, second, hidden, both,
-    gmid, gbranch, gmixed, gjoint, gfirst, dsb, dq, dk, dv, sem_a, sem_b, sem_c, sem_d, sem_l, sem_x, sem_z,
+    gains, g_gain, factor, stats, lifted, first, inv1, normed, q, k, v, *rest,
 ):
     knock()
-    prob = (p0, p1, p2, p3)
+    prob = rest[: LEN // BLOCK]
+    (
+        sbuf, rl, osum, mixed, middle, second, hidden, both, gmid, gbranch, gmixed, gjoint, gfirst, dsb, dq, dk, dv, sem_a, sem_b, sem_c, sem_d, sem_l, sem_x, sem_z,
+    ) = rest[LEN // BLOCK :]
     loads = [
         pltpu.make_async_copy(src, dst, sem_l.at[i])
         for i, (src, dst) in enumerate(
@@ -479,9 +516,12 @@
     ]
     for load in loads:
         load.start()
-    for load in loads[:6]:
-        load.wait()
-    own_tiles(w_in, w_qkv, w_out, w_gu, w_down, gains_own, tile_a, tile_b, flat_b.at[pl.ds(0, B_ROWS)])
+
+    def tiles():
+        for load in loads[:6]:
+            load.wait()
+        own_tiles(w_in, w_qkv, w_out, w_gu, w_down, gains_own, tile_a, tile_b, flat_b.at[pl.ds(0, B_ROWS)])
+
     a, b = GatherDirect(tile_a, all_a, sem_a), Gather(tile_b, all_b, sem_b)
 
     def scalars():
@@ -496,10 +536,11 @@
         for s in (0, 1):
             lifted[s] = (feats[s].astype(f32) * factor[:F, s : s + 1]).astype(bf16)
 
-    enter(sem_x, sem_z, a.to, (scalars, lift))
+    enter(sem_x, sem_z, a.to, (tiles, scalars, lift))
+    b.first()
     a.second()
-    b.first()
     a.last()
+    b.second()
     flat_a[...] = all_a[...].reshape(128 * A_ROWS, 128)
     gain_columns(flat_a, gains)
 
@@ -539,15 +580,11 @@
                 ref[s, :, :, t] = (jnp.concatenate([u * c - w * sn, w * c + u * sn], axis=1) * scale).astype(bf16)
             v[s, :, :, t] = joint[2].astype(bf16)
 
-    b.second()
-
-    @pl.loop(0, 2)
-    def _(s):
-        @pl.loop(0, H // GROUP)
-        def _(hh):
-            attend(s, hh, q, k, v, prob, sbuf, rl, osum, mixed)
-
-        @pl.when(s == 0)
+    @pl.loop(0, H // GROUP)
+    def _(hh):
+        attend(hh, q, k, v, prob, sbuf, rl, osum, mixed)
+
+        @pl.when(hh == 0)
         def _():
             b.third()
 
@@ -601,13 +638,11 @@
     a, b = ReduceDirect(all_a, half_a, row_a, sem_c), Reduce(all_b, half_b, row_b, line_b, sem_d)
     b.first()
 
-    @pl.loop(0, 2)
-    def _(s):
-        @pl.loop(0, H // GROUP)
-        def _(hh):
-            attend_back(s, hh, q, k, v, prob, rl, osum, gmixed, cosr, sinr, gjoint, dsb, dq, dk, dv)
-
-        @pl.when(s == 0)
+    @pl.loop(0, H // GROUP)
+    def _(hh):
+        attend_back(hh, q, k, v, prob, rl, osum, gmixed, cosr, sinr, gjoint, dsb, dq, dk, dv)
+
+        @pl.when(hh == 0)
         def _():
             b.second()
 
@@ -676,11 +711,11 @@
             V((D, 2), f32), V((2, D, 128), f32), V((128, 8), f32), V((1, 128), f32),
             V((2, F, LEN), bf16), V((2, D, LEN), f32), V((2, 1, LEN), f32), V((2, D, LEN), bf16),
             V((2, H, HD, LEN), bf16), V((2, H, HD, LEN), bf16), V((2, H, HD, LEN), bf16),
-            *[V((2, H, (j + 1) * QT, QT), bf16) for j in range(4)],
-            V((2, LEN, QT), f32), V((2, H, 1, LEN), f32), V((2, H, HD, LEN), f32), V((2, H, HD, LEN), bf16),
+            *[V((H, (j + 1) * BLOCK, 2 * BLOCK), bf16) for j in range(LEN // BLOCK)],
+            V((2, LEN, 2 * BLOCK), f32), V((2, H, 1, LEN), f32), V((2, H, HD, LEN), f32), V((2, H, HD, LEN), bf16),
             V((2, D, LEN), f32), V((D, LEN), bf16), V((2, FF, LEN), bf16), V((2 * FF, LEN), bf16),
             V((2, D, LEN), f32), V((D, LEN), bf16), V((2, H, HD, LEN), f32), V((2, 3, H, HD, LEN), bf16), V((2, D, LEN), bf16),
-            V((2, LEN, QT), bf16), *[V((GROUP, HD, LEN), f32)] * 3,
+            V((2, LEN, 2 * BLOCK), bf16), V((GROUP, 2, HD, LEN), f32), *[V((GROUP, 2 * HD, LEN), f32)] * 2,
             *[pltpu.SemaphoreType.DMA((2, 3))] * 4, pltpu.SemaphoreType.DMA((17,)), *[pltpu.SemaphoreType.REGULAR] * 2,
         ],
         compiler_params=pltpu.CompilerParams(collective_id=0, has_side_effects=True, vmem_limit_bytes=63 * 2**20),

time: 79.9 us -> 75.7 us (0.947)
  Pallas kernels: 79 us -> 74.7 us
    pallas_call x1, Pallas kernels: 76.2 us -> 71.9 us  [run_layer(): pl.pallas_call(layer_kernel, in_specs=[HB] * 15, out_specs=[HB, HB, VM, V...]
where the time goes in v1:
time: 75.7 us; the launch traced here: 75.5 us
  Pallas kernels  74.7 us (99%)
  between operations  0.82 us (1%)
    pallas_call x1, Pallas kernels, run_layer(): pl.pallas_call(layer_kernel, in_specs=[HB] * 15, out_specs=[HB, HB, VM, V...  71.9 us
    pallas_call x1, Pallas kernels, hand_out(): pl.pallas_call(finish_kernel, in_specs=[HB] * 5, out_specs=[HB, HB] + [VM...  2.81 us

profile of v1, /device:TPU:1, one launch (start us, length us, event | category | flops | bytes accessed | tf_op | source)
XLA Modules:
  0.0 75.5 jit_solution(3476402021685851883)
XLA Ops:
  0.6 71.9 %shard_map.223 = (bf16[2,144,1024]{2,1,0:T(8,128)(2,1)}, bf16[2,96,1024]{2,1,0:T(8,128)(2,1)}, f32[8,128]{1,0:T(8,128)}, f32[16,128]{1,0:T(8,128)}) custom-call(bf16[2,96,1024]{2,1,0:T(8,128)(2,1)} %bitcast.5, f32[2,1024]{1,0:T(2,128)} %targets_h.1, s32[2,84]{1,0:T(2,128)} %lag_h.1, s32[2,12]{1,0:T(2,128)} %date_h.1, s32[2]{0:T(128)} %freq_h.1, s32[2]{0:T(128)} %sets_h.1, ...), custom_call_target="tpu_custom_call" | custom-call | tf_op jit(solution)/shard_map/pallas_call | solution.py:694
  72.5 2.8 %shard_map.224 = (bf16[2,144,1024]{2,1,0:T(8,128)(2,1)}, bf16[2,96,1024]{2,1,0:T(8,128)(2,1)}, f32[108]{0:T(128)}, f32[486]{0:T(512)}, f32[162]{0:T(256)}, /*ind...) custom-call(bf16[2,144,1024]{2,1,0:T(8,128)(2,1)} %get-tuple-element.22.out_h, ...), custom_call_target="tpu_custom_call" | custom-call | tf_op jit(solution)/shard_map/pallas_call | solution.py:751

commit v2 on v1

--- a/solution.py
+++ b/solution.py
@@ -549,7 +549,8 @@
         for t, at, width in lane_tiles(SPECS[name][0]):
             val = mat[t][:, :width]
             out[:, at : at + width] = val.astype(bf16)
-            outT[at : at + width, :] = val.T.astype(bf16)
+            down = at if name != "gu" else 2 * at if at < FF else 2 * (at - FF) + 128
+            outT[down : down + width, :] = val.T.astype(bf16)
         mat[...] = jnp.zeros_like(mat)
 
     emit("in", flat_a, A_ROWS, m_in, win, winT)
@@ -605,15 +606,17 @@
             sec = (mid * r * gain1).astype(bf16)
             second[:, t] = sec
             g = dout[s, :, t]
-            for f in range(0, FF, 128):
-                gate = dot(wguT[f : f + 128], sec)
-                up = dot(wguT[FF + f : FF + f + 128], sec)
-                gh = dot(wdown[f : f + 128], g)
-                sig = 1.0 / (1.0 + jnp.exp(-gate))
-                silu = gate * sig
-                hidden[s, f : f + 128, t] = (silu * up).astype(bf16)
-                both[FF + f : FF + f + 128, t] = (gh * silu).astype(bf16)
-                both[f : f + 128, t] = (gh * up * (sig + silu * (1.0 - sig))).astype(bf16)
+            for c in range(0, LEN, 256):
+                for f in range(0, FF, 128):
+                    part = slice(c, c + 256)
+                    x = dot(wguT[2 * f : 2 * f + 256], sec[:, part])
+                    gate, up = x[:128], x[128:]
+                    gh = dot(wdown[f : f + 128], g[:, part])
+                    sig = 1.0 / (1.0 + jnp.exp(-gate))
+                    silu = gate * sig
+                    hidden[s, f : f + 128, part] = (silu * up).astype(bf16)
+                    both[FF + f : FF + f + 128, part] = (gh * silu).astype(bf16)
+                    both[f : f + 128, part] = (gh * up * (sig + silu * (1.0 - sig))).astype(bf16)
             middle[s, :, t] = mid
             c = dot(wgu[...], both[:, t])
             cg = c * gain1

time: 75.7 us -> 75 us (level)
  no operation moved by 1% of the time
where the time goes in v2:
time: 75 us; the launch traced here: 74.8 us
  Pallas kernels  74 us (99%)
  between operations  0.82 us (1%)
    pallas_call x1, Pallas kernels, run_layer(): pl.pallas_call(layer_kernel, in_specs=[HB] * 15, out_specs=[HB, HB, VM, V...  71.2 us
    pallas_call x1, Pallas kernels, hand_out(): pl.pallas_call(finish_kernel, in_specs=[HB] * 5, out_specs=[HB, HB] + [VM...  2.81 us

profile of v2, /device:TPU:1, one launch (start us, length us, event | category | flops | bytes accessed | tf_op | source)
XLA Modules:
  0.0 74.8 jit_solution(17497366363753090704)
XLA Ops:
  0.6 71.2 %shard_map.223 = (bf16[2,144,1024]{2,1,0:T(8,128)(2,1)}, bf16[2,96,1024]{2,1,0:T(8,128)(2,1)}, f32[8,128]{1,0:T(8,128)}, f32[16,128]{1,0:T(8,128)}) custom-call(bf16[2,96,1024]{2,1,0:T(8,128)(2,1)} %bitcast.5, f32[2,1024]{1,0:T(2,128)} %targets_h.1, s32[2,84]{1,0:T(2,128)} %lag_h.1, s32[2,12]{1,0:T(2,128)} %date_h.1, s32[2]{0:T(128)} %freq_h.1, s32[2]{0:T(128)} %sets_h.1, ...), custom_call_target="tpu_custom_call" | custom-call | tf_op jit(solution)/shard_map/pallas_call | solution.py:697
  71.9 2.8 %shard_map.224 = (bf16[2,144,1024]{2,1,0:T(8,128)(2,1)}, bf16[2,96,1024]{2,1,0:T(8,128)(2,1)}, f32[108]{0:T(128)}, f32[486]{0:T(512)}, f32[162]{0:T(256)}, /*ind...) custom-call(bf16[2,144,1024]{2,1,0:T(8,128)(2,1)} %get-tuple-element.22.out_h, ...), custom_call_target="tpu_custom_call" | custom-call | tf_op jit(solution)/shard_map/pallas_call | solution.py:754
